TPU v7x, 256 devices: a whole 4x4x8 slice. The times are simulated.
256 devices in a mesh: store: 64 (over z, y, core), tp: 4 (over x).
Axes of the slice: x: 4, y: 4, z: 8, core: 2. Of those that a mesh axis runs over, the one named last changes fastest.
Arguments:
- slot_anchor: bfloat16 [81920, 8, 256], P(('store', 'tp')), may hold values from -6 to 6
- slot_delta: bfloat16 [81920, 4, 8, 256], P(('store', 'tp')), may hold values from -6 to 6
- slot_scale: bfloat16 [81920, 8, 2], P(('store', 'tp')), may hold values from 0.25 to 1
- send_slot: int32 [256, 64, 5], P(('store', 'tp')), may hold values from -1 to 319, as said below
- recv_block: int32 [64, 256, 5], P('store'), may hold values from -1 to 1023, as said below
- turn_queries: bfloat16 [8192, 8, 1024], P(('store', 'tp')), may hold values from -28 to 28
- turn_kv: bfloat16 [8192, 8, 256], P(('store', 'tp')), may hold values from -9 to 9
Outputs:
- cache_out: bfloat16 [64, 4224, 8, 256], P('store', None, 'tp')
- attended: bfloat16 [8192, 8, 1024], P(('store', 'tp'))
Inputs may be any that keep to these rules, and one draw needn't show every extreme that they name: Holder g sends its slot send_slot[g, o, c] as place c to session o, -1 for none; no slot of a holder is named twice; for each holder and session the named places come first; at most 5 named places for one holder and one session, and every session has some holder with 5. recv_block[o, g, c] is -1 exactly where send_slot[g, o, c] is -1; every block 0 to 1023 of a session is named exactly once.
All inputs are finite; a program needn't handle non-finite values.
Results may differ from a plain program's by a relative error of at most 0.0082.
Values may be sent and summed in bfloat16 or wider, within the bound.
A program may use at most 128 MiB of HBM per device.

v0:
```python
import math

import jax
import jax.numpy as jnp
from jax import lax
from jax.sharding import PartitionSpec as P

CTX = 4096
NBLK = 1024


def decode_rows(anchors, deltas, scales):
    head_size = deltas.shape[-1] // 2
    spread = jnp.repeat(scales.astype(jnp.float32), head_size, axis=-1)
    return (anchors.astype(jnp.float32) + spread * deltas.astype(jnp.float32)).astype(jnp.bfloat16)


def attend_local(queries, restored, context):
    head_size = restored.shape[-1] // 2
    turn_length = queries.shape[0]
    local_heads = restored.shape[1]
    query_count = queries.shape[2] // head_size
    positions = jnp.arange(restored.shape[0])[None, :]
    limits = context + 1 + jnp.arange(turn_length * query_count)[:, None] // query_count
    allowed = positions < limits
    results = []
    for head_index in range(local_heads):
        key_rows = restored[:, head_index, :head_size]
        value_rows = restored[:, head_index, head_size:]
        query_rows = queries[:, head_index, :].reshape(turn_length * query_count, head_size)
        scores = lax.dot_general(
            query_rows, key_rows, (((1,), (1,)), ((), ())), preferred_element_type=jnp.float32
        ) * (1.0 / math.sqrt(head_size))
        scores = jnp.where(allowed, scores, -jnp.inf)
        row_max = jnp.max(scores, axis=-1, keepdims=True)
        powers = jnp.exp(scores - row_max)
        row_total = jnp.sum(powers, axis=-1, keepdims=True)
        weights = (powers / row_total).astype(jnp.bfloat16)
        mixture = jnp.dot(weights, value_rows, preferred_element_type=jnp.float32).astype(
            jnp.bfloat16
        )
        results.append(mixture.reshape(turn_length, query_count * head_size))
    return jnp.stack(results, axis=1)


def shards(slot_anchor, slot_delta, slot_scale, send_slot, recv_block, turn_queries, turn_kv):
    queries, turn_rows = (
        lax.all_to_all(turn_queries, "tp", split_axis=1, concat_axis=0, tiled=True),
        lax.all_to_all(turn_kv, "tp", split_axis=1, concat_axis=0, tiled=True),
    )
    slot_index = send_slot[0]
    safe_slot = jnp.maximum(slot_index, 0)
    anchors = slot_anchor[safe_slot][:, :, None]
    deltas = slot_delta[safe_slot]
    scales = slot_scale[safe_slot][:, :, None]
    moved_anchor, moved_delta, moved_scale = (
        lax.all_to_all(
            lax.all_to_all(anchors, "store", split_axis=0, concat_axis=0, tiled=True),
            "tp",
            split_axis=3,
            concat_axis=3,
            tiled=True,
        ),
        lax.all_to_all(
            lax.all_to_all(deltas, "store", split_axis=0, concat_axis=0, tiled=True),
            "tp",
            split_axis=3,
            concat_axis=3,
            tiled=True,
        ),
        lax.all_to_all(
            lax.all_to_all(scales, "store", split_axis=0, concat_axis=0, tiled=True),
            "tp",
            split_axis=3,
            concat_axis=3,
            tiled=True,
        ),
    )
    arrived = decode_rows(moved_anchor, moved_delta, moved_scale)
    sources = arrived.shape[0]
    capacity = arrived.shape[1]
    block_length = arrived.shape[2]
    tp_count = lax.axis_size("tp")
    local_heads = arrived.shape[3] // tp_count
    row_width = arrived.shape[4]
    arrived = arrived.reshape(sources, capacity, block_length, tp_count, local_heads, row_width)
    block_ids = recv_block[0].reshape(sources, tp_count, capacity)
    target = jnp.where(block_ids >= 0, block_ids, NBLK).transpose(0, 2, 1)[:, :, None, :, None]
    offsets = jnp.arange(block_length)[None, None, :, None, None]
    head_slots = jnp.arange(local_heads)[None, None, None, None, :]
    cache_rows = jnp.zeros((NBLK, block_length, local_heads, row_width), jnp.bfloat16)
    cache_rows = cache_rows.at[target, offsets, head_slots].set(arrived, mode="drop")
    restored = jnp.concatenate([cache_rows.reshape(CTX, local_heads, row_width), turn_rows], axis=0)
    attended = attend_local(queries, restored, CTX)
    result = lax.all_to_all(attended, "tp", split_axis=0, concat_axis=1, tiled=True)
    return (restored[None], result)


def solution(mesh):
    placed = (
        P(("store", "tp"), None, None),
        P(("store", "tp"), None, None, None),
        P(("store", "tp"), None, None),
        P(("store", "tp"), None, None),
        P("store", None, None),
        P(("store", "tp"), None, None),
        P(("store", "tp"), None, None),
    )
    return jax.shard_map(
        shards,
        mesh=mesh,
        in_specs=placed,
        out_specs=(P("store", None, "tp", None), P(("store", "tp"), None, None)),
        check_vma=False,
    )
```

profile of v0, /device:TPU:58, one launch (start us, length us, event | category | flops | bytes accessed | tf_op | source)
XLA Modules:
  0.0 472.0 jit_solution(13797073757576134711)
XLA Ops:
  4.6 20.8 %all_to_all.84 = bf16[64,5,1,8,2]{3,4,2,1,0:T(2,128)(2,1)S(1)} all-to-all(bf16[64,5,1,8,2]{3,4,2,1,0:T(2,128)(2,1)S(1)} %bitcast.65), channel_id=1, replica_groups=mesh['store'=64,'tp'=4] {'store'}, dimensions={0} | all-to-all | bytes 20480 | tf_op jit(solution)/shard_map/all_to_all | solution.py:72
  26.2 4.8 %all-to-all-start.3 = ((bf16[4,2,640]{2,1,0:T(2,128)(2,1)}), bf16[4,2,640]{2,1,0:T(2,128)(2,1)S(1)}, u32[]{:S(2)}, u32[]{:S(2)}) async-start(bf16[4,2,640]{2,1,0:T(2,128)(2,1)} %reshape.136), calls=%async_computation.3 | async-start | bytes 20480 | tf_op jit(solution)/shard_map/all_to_all | solution.py:71
  34.9 4.8 %all-to-all-start.6 = ((bf16[32,8,256]{2,0,1:T(8,128)(2,1)}), bf16[32,8,256]{2,0,1:T(8,128)(2,1)S(1)}, u32[]{:S(2)}, u32[]{:S(2)}) async-start(bf16[32,8,256]{2,0,1:T(8,128)(2,1)} %copy.96), calls=%async_computation.6 | async-start | bytes 262144 | tf_op jit(solution)/shard_map/all_to_all | solution.py:49
  41.7 2.4 all-to-all-done.6
  44.1 4.9 %all-to-all-start.7 = ((bf16[32,8,1024]{2,0,1:T(8,128)(2,1)}), bf16[32,8,1024]{2,0,1:T(8,128)(2,1)S(1)}, u32[]{:S(2)}, u32[]{:S(2)}) async-start(bf16[32,8,1024]{2,0,1:T(8,128)(2,1)} %copy.98), calls=%async_computation.7 | async-start | bytes 1048576 | tf_op jit(solution)/shard_map/all_to_all | solution.py:48
  49.0 2.5 gather_fusion
  51.5 4.2 all-to-all-done.7
  55.7 6.7 %all-to-all-start = ((bf16[64,5,1,8,256]{4,3,1,2,0:T(8,128)(2,1)}), bf16[64,5,1,8,256]{4,3,1,2,0:T(8,128)(2,1)S(1)}, u32[]{:S(2)}, u32[]{:S(2)}) async-start(bf16[64,5,1,8,256]{4,3,1,2,0:T(8,128)(2,1)} %bitcast.1), calls=%async_computation | async-start | bytes 2621440 | tf_op jit(solution)/shard_map/all_to_all | solution.py:58
  62.4 6.1 %gather_fusion.2 = bf16[320,4,8,256]{3,2,1,0:T(8,128)(2,1)} fusion(bf16[320,4,8,256]{3,2,1,0:T(8,128)(2,1)} %param.8, s32[1024]{0:T(1024)S(1)} %pad_clamp_fusion), kind=kCustom, calls=%fused_computation.2 | custom fusion | bytes 10487040 | tf_op jit(solution)/shard_map/gather | solution.py:54
  68.5 7.6 %copy.93 = bf16[64,5,4,8,256]{4,2,1,3,0:T(4,128)(2,1)} copy(bf16[64,5,4,8,256]{4,3,2,1,0:T(8,128)(2,1)} %bitcast.63) | data formatting | bytes 10485760 | tf_op jit(solution)/shard_map/gather | solution.py:54
  76.0 20.0 %all-to-all-done = bf16[64,5,1,8,256]{4,3,1,2,0:T(8,128)(2,1)S(1)} async-done(((bf16[64,5,1,8,256]{4,3,1,2,0:T(8,128)(2,1)}), bf16[64,5,1,8,256]{4,3,1,2,0:T(8,128)(2,1)S(1)}, u32[]{:S(2)}, u32[]{:S(2)}) %all-to-all-start) | async-done | bytes 1310752 | tf_op jit(solution)/shard_map/all_to_all | solution.py:58
  96.0 6.6 %all-to-all-start.4 = ((bf16[64,5,4,8,256]{4,2,1,3,0:T(4,128)(2,1)}), bf16[64,5,4,8,256]{4,2,1,3,0:T(4,128)(2,1)}, u32[]{:S(2)}, u32[]{:S(2)}) async-start(bf16[64,5,4,8,256]{4,2,1,3,0:T(4,128)(2,1)} %copy.93), calls=%async_computation.4 | async-start | bytes 10485760 | tf_op jit(solution)/shard_map/all_to_all | solution.py:65
  103.9 116.5 %all-to-all-done.4 = bf16[64,5,4,8,256]{4,2,1,3,0:T(4,128)(2,1)} async-done(((bf16[64,5,4,8,256]{4,2,1,3,0:T(4,128)(2,1)}), bf16[64,5,4,8,256]{4,2,1,3,0:T(4,128)(2,1)}, u32[]{:S(2)}, u32[]{:S(2)}) %all-to-all-start.4) | async-done | bytes 5242912 | tf_op jit(solution)/shard_map/all_to_all | solution.py:65
  220.5 5.0 %all-to-all-start.1 = ((bf16[64,5,1,8,256]{4,0,2,1,3:T(8,128)(2,1)}), bf16[64,5,1,8,256]{4,0,2,1,3:T(8,128)(2,1)S(1)}, u32[]{:S(2)}, u32[]{:S(2)}) async-start(bf16[64,5,1,8,256]{4,0,2,1,3:T(8,128)(2,1)} %copy.86), calls=%async_computation.1 | async-start | bytes 2621440 | tf_op jit(solution)/shard_map/all_to_all | solution.py:57
  225.4 6.6 %copy.94 = bf16[64,5,4,8,256]{4,2,1,0,3:T(4,128)(2,1)} copy(bf16[64,5,4,8,256]{4,2,1,3,0:T(4,128)(2,1)} %all-to-all-done.4) | data formatting | bytes 10485760 | tf_op jit(solution)/shard_map/all_to_all | solution.py:65
  232.1 10.2 %all-to-all-done.1 = bf16[64,5,1,8,256]{4,0,2,1,3:T(8,128)(2,1)S(1)} async-done(((bf16[64,5,1,8,256]{4,0,2,1,3:T(8,128)(2,1)}), bf16[64,5,1,8,256]{4,0,2,1,3:T(8,128)(2,1)S(1)}, u32[]{:S(2)}, u32[]{:S(2)}) %all-to-all-start.1) | async-done | bytes 1310752 | tf_op jit(solution)/shard_map/all_to_all | solution.py:57
  242.3 6.6 %all-to-all-start.5 = ((bf16[64,5,4,8,256]{4,2,1,0,3:T(4,128)(2,1)}), bf16[64,5,4,8,256]{4,2,1,0,3:T(4,128)(2,1)}, u32[]{:S(2)}, u32[]{:S(2)}) async-start(bf16[64,5,4,8,256]{4,2,1,0,3:T(4,128)(2,1)} %copy.94), calls=%async_computation.5 | async-start | bytes 10485760 | tf_op jit(solution)/shard_map/all_to_all | solution.py:64
  251.8 3.5 reshape.118
  260.5 3.0 copy.87
  263.5 43.6 %all-to-all-done.5 = bf16[64,5,4,8,256]{4,2,1,0,3:T(4,128)(2,1)} async-done(((bf16[64,5,4,8,256]{4,2,1,0,3:T(4,128)(2,1)}), bf16[64,5,4,8,256]{4,2,1,0,3:T(4,128)(2,1)}, u32[]{:S(2)}, u32[]{:S(2)}) %all-to-all-start.5) | async-done | bytes 5242912 | tf_op jit(solution)/shard_map/all_to_all | solution.py:64
  307.1 12.8 %add_convert_fusion = bf16[64,5,4,8,256]{4,3,2,1,0:T(8,128)(2,1)} fusion(bf16[64,5,4,8,256]{4,2,1,0,3:T(4,128)(2,1)} %all-to-all-done.5, f32[64,5,8,256]{3,2,1,0:T(8,128)} %broadcast_bitcast_fusion, f32[64,5,8,256]{3,2,1,0:T(8,128)} %copy.87), kind=kLoop, calls=%fused_computation.13 | loop fusion | flops 10485760 | bytes 15728640 | tf_op jit(solution)/shard_map/convert_element_type | solution.py:15
  320.0 46.7 %scatter_custom_fusion = bf16[8192,256]{1,0:T(8,128)(2,1)} fusion(s32[10240]{0:T(1024)S(1)} %reshape.118, bf16[10240,256]{1,0:T(8,128)(2,1)} %bitcast.64, bf16[]{:T(256)} %constant.13.clone.1), kind=kCustom, calls=%fused_computation.26 | custom fusion | bytes 4194816
  366.7 7.2 %reshape.86 = bf16[4096,2,256]{2,1,0:T(2,128)(2,1)} reshape(bf16[8192,256]{1,0:T(8,128)(2,1)} %scatter_custom_fusion) | data formatting | bytes 8388608 | tf_op jit(solution)/shard_map/reshape | solution.py:93
  373.9 25.2 %fusion.6 = (bf16[4224,1,128]{2,1,0:T(2,128)(2,1)}, bf16[4224,1,128]{2,1,0:T(2,128)(2,1)S(1)}, bf16[4224,1,128]{2,1,0:T(2,128)(2,1)}, bf16[4224,1,128]{2,1,0:T(2,128)(2,1)S(1)}) fusion(bf16[128,2,256]{2,1,0:T(2,128)(2,1)S(1)} %bitcast.70, bf16[4096,2,256]{2,1,0:T(2,128)(2,1)} %reshape.86), kind=kLoop, calls=%fused_computation.23 | loop fusion | flops 2162688 | bytes 8650752 | tf_op jit(solution)/shard_map/concatenate | solution.py:93
  399.1 7.5 %fusion.28 = (f32[1024]{0:T(1024)S(1)}, f32[1024,4224]{0,1:T(8,128)}) fusion(bf16[1024,128]{1,0:T(8,128)(2,1)S(1)} %copy-done.4, bf16[4224,1,128]{2,1,0:T(2,128)(2,1)S(1)} %get-tuple-element.5, s32[1024]{0:T(1024)S(1)} %fusion.22), kind=kOutput, calls=%fused_computation.61 | convolution fusion | flops 1124596736 | bytes 18653184 | tf_op jit(solution)/shard_map/dot_general | solution.py:31
  406.6 8.2 %fusion = f32[1024]{0:T(1024)S(1)} fusion(f32[1024,4224]{0,1:T(8,128)} %get-tuple-element.13, f32[1024]{0:T(1024)S(1)} %get-tuple-element.12), kind=kLoop, calls=%fused_computation.11 | loop fusion | flops 8649728 | bytes 17309696 | tf_op jit(solution)/shard_map/reduce_sum | solution.py:37
  414.9 9.6 %fusion.12 = bf16[1024,128]{1,0:T(8,128)(2,1)S(1)} fusion(f32[1024,4224]{0,1:T(8,128)} %get-tuple-element.13, f32[1024]{0:T(1024)S(1)} %fusion, f32[1024]{0:T(1024)S(1)} %get-tuple-element.12, bf16[4224,1,128]{2,1,0:T(2,128)(2,1)} %get-tuple-element.4), kind=kOutput, calls=%fused_computation.31 | convolution fusion | flops 1120403456 | bytes 18653184 | tf_op jit(solution)/shard_map/dot_general | solution.py:39
  424.6 9.2 %fusion.27 = (f32[1024]{0:T(1024)S(1)}, f32[1024,4224]{0,1:T(8,128)}) fusion(bf16[1024,128]{1,0:T(8,128)(2,1)S(1)} %copy-done.3, bf16[4224,1,128]{2,1,0:T(2,128)(2,1)} %get-tuple-element.6, s32[1024]{0:T(1024)S(1)} %fusion.22), kind=kOutput, calls=%fused_computation.60 | convolution fusion | flops 1124596736 | bytes 18653184 | tf_op jit(solution)/shard_map/dot_general | solution.py:31
  433.9 8.2 %fusion.1 = f32[1024]{0:T(1024)S(1)} fusion(f32[1024,4224]{0,1:T(8,128)} %get-tuple-element.11, f32[1024]{0:T(1024)S(1)} %get-tuple-element.10), kind=kLoop, calls=%fused_computation.12 | loop fusion | flops 8649728 | bytes 17309696 | tf_op jit(solution)/shard_map/reduce_sum | solution.py:37
  442.1 7.5 %fusion.11 = bf16[1024,128]{1,0:T(8,128)(2,1)S(1)} fusion(f32[1024,4224]{0,1:T(8,128)} %get-tuple-element.11, f32[1024]{0:T(1024)S(1)} %fusion.1, f32[1024]{0:T(1024)S(1)} %get-tuple-element.10, bf16[4224,1,128]{2,1,0:T(2,128)(2,1)S(1)} %get-tuple-element.7), kind=kOutput, calls=%fused_computation.30 | convolution fusion | flops 1120403456 | bytes 18653184 | tf_op jit(solution)/shard_map/dot_general | solution.py:39
  451.8 4.9 %all-to-all-start.8 = ((bf16[128,2,1024]{2,1,0:T(2,128)(2,1)}), bf16[128,2,1024]{2,1,0:T(2,128)(2,1)S(1)}, u32[]{:S(2)}, u32[]{:S(2)}) async-start(bf16[128,2,1024]{2,1,0:T(2,128)(2,1)} %pad_maximum_fusion.1), calls=%async_computation.8 | async-start | bytes 1048576 | tf_op jit(solution)/shard_map/all_to_all | solution.py:95
  456.7 13.3 %fusion.4 = bf16[1,4224,2,256]{3,2,1,0:T(2,128)(2,1)} fusion(bf16[128,2,256]{2,1,0:T(2,128)(2,1)} %bitcast.69, bf16[4096,2,256]{2,1,0:T(2,128)(2,1)} %reshape.86), kind=kLoop, calls=%fused_computation.21 | loop fusion | flops 2162688 | bytes 8650752 | tf_op jit(solution)/shard_map/broadcast_in_dim | solution.py:96
  (56 shorter events, 23.8 us)
Async XLA Ops:
  0.6 48.4 %copy-start = (bf16[320,8,256]{2,1,0:T(8,128)(2,1)S(1)}, bf16[320,8,256]{2,1,0:T(8,128)(2,1)}, u32[]{:S(2)}) copy-start(bf16[320,8,256]{2,1,0:T(8,128)(2,1)} %param.7) | copy-start | bytes 3932164
  26.2 8.7 %all-to-all-start.3 = ((bf16[4,2,640]{2,1,0:T(2,128)(2,1)}), bf16[4,2,640]{2,1,0:T(2,128)(2,1)S(1)}, u32[]{:S(2)}, u32[]{:S(2)}) async-start(bf16[4,2,640]{2,1,0:T(2,128)(2,1)} %reshape.136), calls=%async_computation.3 | async-start | bytes 20480 | tf_op jit(solution)/shard_map/all_to_all | solution.py:71
  34.9 9.3 %all-to-all-start.6 = ((bf16[32,8,256]{2,0,1:T(8,128)(2,1)}), bf16[32,8,256]{2,0,1:T(8,128)(2,1)S(1)}, u32[]{:S(2)}, u32[]{:S(2)}) async-start(bf16[32,8,256]{2,0,1:T(8,128)(2,1)} %copy.96), calls=%async_computation.6 | async-start | bytes 262144 | tf_op jit(solution)/shard_map/all_to_all | solution.py:49
  44.1 11.5 %all-to-all-start.7 = ((bf16[32,8,1024]{2,0,1:T(8,128)(2,1)}), bf16[32,8,1024]{2,0,1:T(8,128)(2,1)S(1)}, u32[]{:S(2)}, u32[]{:S(2)}) async-start(bf16[32,8,1024]{2,0,1:T(8,128)(2,1)} %copy.98), calls=%async_computation.7 | async-start | bytes 1048576 | tf_op jit(solution)/shard_map/all_to_all | solution.py:48
  55.7 40.4 %all-to-all-start = ((bf16[64,5,1,8,256]{4,3,1,2,0:T(8,128)(2,1)}), bf16[64,5,1,8,256]{4,3,1,2,0:T(8,128)(2,1)S(1)}, u32[]{:S(2)}, u32[]{:S(2)}) async-start(bf16[64,5,1,8,256]{4,3,1,2,0:T(8,128)(2,1)} %bitcast.1), calls=%async_computation | async-start | bytes 2621440 | tf_op jit(solution)/shard_map/all_to_all | solution.py:58
  96.0 124.4 %all-to-all-start.4 = ((bf16[64,5,4,8,256]{4,2,1,3,0:T(4,128)(2,1)}), bf16[64,5,4,8,256]{4,2,1,3,0:T(4,128)(2,1)}, u32[]{:S(2)}, u32[]{:S(2)}) async-start(bf16[64,5,4,8,256]{4,2,1,3,0:T(4,128)(2,1)} %copy.93), calls=%async_computation.4 | async-start | bytes 10485760 | tf_op jit(solution)/shard_map/all_to_all | solution.py:65
  220.5 21.8 %all-to-all-start.1 = ((bf16[64,5,1,8,256]{4,0,2,1,3:T(8,128)(2,1)}), bf16[64,5,1,8,256]{4,0,2,1,3:T(8,128)(2,1)S(1)}, u32[]{:S(2)}, u32[]{:S(2)}) async-start(bf16[64,5,1,8,256]{4,0,2,1,3:T(8,128)(2,1)} %copy.86), calls=%async_computation.1 | async-start | bytes 2621440 | tf_op jit(solution)/shard_map/all_to_all | solution.py:57
  232.0 16.9 %copy-start.5 = (s32[1,256,5]{1,0,2:T(1,128)S(1)}, s32[1,256,5]{1,0,2:T(1,128)}, u32[]{:S(2)}) copy-start(s32[1,256,5]{1,0,2:T(1,128)} %param.11) | copy-start | bytes 15364
  232.0 17.3 %copy-start.7 = (s32[3]{0:T(128)S(1)}, s32[3]{0:T(128)}, u32[]{:S(2)}) copy-start(s32[3]{0:T(128)} %constant.49) | copy-start | bytes 40
  232.0 17.5 %copy-start.6 = (s32[3]{0:T(128)S(1)}, s32[3]{0:T(128)}, u32[]{:S(2)}) copy-start(s32[3]{0:T(128)} %constant.52) | copy-start | bytes 40
  242.3 64.9 %all-to-all-start.5 = ((bf16[64,5,4,8,256]{4,2,1,0,3:T(4,128)(2,1)}), bf16[64,5,4,8,256]{4,2,1,0,3:T(4,128)(2,1)}, u32[]{:S(2)}, u32[]{:S(2)}) async-start(bf16[64,5,4,8,256]{4,2,1,0,3:T(4,128)(2,1)} %copy.94), calls=%async_computation.5 | async-start | bytes 10485760 | tf_op jit(solution)/shard_map/all_to_all | solution.py:64
  366.7 7.2 %copy-start.2 = (bf16[32,4,2,256]{3,2,0,1:T(2,128)(2,1)S(1)}, bf16[32,4,2,256]{3,2,0,1:T(2,128)(2,1)}, u32[]{:S(2)}) copy-start(bf16[32,4,2,256]{3,2,0,1:T(2,128)(2,1)} %copy.97) | copy-start | bytes 393220
  373.9 25.2 %copy-start.4 = (bf16[1024,128]{1,0:T(8,128)(2,1)S(1)}, bf16[1024,128]{1,0:T(8,128)(2,1)}, u32[]{:S(2)}) copy-start(bf16[1024,128]{1,0:T(8,128)(2,1)} %reshape_squeeze.10) | copy-start | bytes 786436
  414.9 9.7 %copy-start.3 = (bf16[1024,128]{1,0:T(8,128)(2,1)S(1)}, bf16[1024,128]{1,0:T(8,128)(2,1)}, u32[]{:S(2)}) copy-start(bf16[1024,128]{1,0:T(8,128)(2,1)} %reshape_squeeze.11) | copy-start | bytes 786436
  451.8 18.2 %all-to-all-start.8 = ((bf16[128,2,1024]{2,1,0:T(2,128)(2,1)}), bf16[128,2,1024]{2,1,0:T(2,128)(2,1)S(1)}, u32[]{:S(2)}, u32[]{:S(2)}) async-start(bf16[128,2,1024]{2,1,0:T(2,128)(2,1)} %pad_maximum_fusion.1), calls=%async_computation.8 | async-start | bytes 1048576 | tf_op jit(solution)/shard_map/all_to_all | solution.py:95
  456.7 14.9 %copy-start.1 = (bf16[320,8,256]{2,1,0:T(8,128)(2,1)S(1)}, bf16[320,8,256]{2,1,0:T(8,128)(2,1)}, u32[]{:S(2)}) copy-start(bf16[320,8,256]{2,1,0:T(8,128)(2,1)} %param.7) | copy-start | bytes 3932164
where the time goes:
time: 481 us; the launch traced here: 472 us
  waiting for transfers between devices  199 us (41%)
  local copies, waits for them, and re-layouts  101 us (21%)
  other arithmetic  71.4 us (15%)
  starting transfers between devices  44.3 us (9%)
  matrix products  33.9 us (7%)
  blocking collectives  20.8 us (4%)
    all_to_all x1, waiting for transfers between devices, shards(): lax.all_to_all(deltas, 'store', split_axis=0, concat_axis=0, tiled=True)  117 us
    unnamed x24, local copies, waits for them, and re-layouts  57.7 us
    all_to_all x1, waiting for transfers between devices, shards(): lax.all_to_all(lax.all_to_all(deltas, 'store', split_axis=0, concat_axis=...  43.6 us
    concatenate x1, other arithmetic, shards(): jnp.concatenate([cache_rows.reshape(CTX, local_heads, row_width), turn_ro...  25.2 us
    all_to_all x1, blocking collectives, shards(): lax.all_to_all(scales, 'store', split_axis=0, concat_axis=0, tiled=True)  20.8 us
    all_to_all x1, waiting for transfers between devices, shards(): lax.all_to_all(anchors, 'store', split_axis=0, concat_axis=0, tiled=True)  20 us
    dot_general x2, matrix products, attend_local(): jnp.dot(weights, value_rows, preferred_element_type=jnp.float32)  17.1 us
    dot_general x2, matrix products, attend_local(): lax.dot_general(query_rows, key_rows, (((1,), (1,)), ((), ())), preferred...  16.8 us
  transfers between devices with their start and end apart: 8, of which 7 were waited for; matrix products, arithmetic and copies ran while one was open for 12% of the time, Pallas kernels for 0%

commit v1 on v0

v1 whole, which is shorter than its diff:
```python
import math

import jax
import jax.numpy as jnp
from jax import lax
from jax.experimental import pallas as pl
from jax.experimental.pallas import tpu as pltpu
from jax.sharding import PartitionSpec as P

MESH = pl.DeviceIdType.MESH
NZ, NY, NC, NX = 8, 4, 2, 4
PLANES = NY * NC
PER_STEP = NZ * NX
CAP = 5
BLK = 4
HD = 128
QPG = 8
NBLK = 1024
TOK = 32
TURN = TOK * NX
HEADS = 2
ROWS = QPG * TOK
KEYS = PER_STEP * CAP * BLK
TURN_TILES = TURN // BLK
SCALE2 = math.log2(math.e) / math.sqrt(HD)
LOW = -1e30


def body(
    anchor_hbm, delta_hbm, scale_ref, slot_ref, inv_ref, bias_ref, q_hbm, kv_hbm,
    cache_hbm, att_hbm,
    anchor_v, delta_v, q_v, kv_v, att_v,
    perm, qf, qsend, qarr, kvsend, kvarr, send, arr,
    flat, keys, values, acc, top, outsend, outarr, stage,
    load_sem, send_sem, recv_sem, turn_send, turn_recv, back_send, back_recv, store_sem,
):
    store = lax.axis_index("store")
    x = lax.axis_index("tp")
    z, y, core = store // (NY * NC), (store // NC) % NY, store % NC

    loads = [
        pltpu.make_async_copy(src, dst, load_sem.at[i])
        for i, (src, dst) in enumerate(
            ((q_hbm, q_v), (kv_hbm, kv_v), (anchor_hbm, anchor_v), (delta_hbm, delta_v))
        )
    ]
    for load in loads:
        load.start()

    barrier = pltpu.get_barrier_semaphore()

    def greet(i, _):
        other = lax.rem(store * NX + x + 1 + i, NZ * NY * NC * NX)
        pl.semaphore_signal(
            barrier, inc=1, device_id=(other // NX, other % NX), device_id_type=MESH
        )
        return 0

    lax.fori_loop(0, NZ * NY * NC * NX - 1, greet, 0)

    out_row = lax.broadcasted_iota(jnp.int32, (64, 64), 0)
    in_row = lax.broadcasted_iota(jnp.int32, (64, 64), 1)
    wanted = ((out_row >> 1) & 7) * 8 + (out_row >> 4) * 2 + (out_row & 1)
    perm[...] = jnp.where(in_row == wanted, 1.0, 0.0).astype(jnp.bfloat16)

    def split(tiles):
        wide = jnp.concatenate(tiles, axis=1).astype(jnp.bfloat16)
        return jnp.dot(perm[...], wide, preferred_element_type=jnp.float32).astype(jnp.bfloat16)

    loads[0].wait()
    for q in range(QPG):
        lanes = q_v[:, :, q * HD : (q + 1) * HD].astype(jnp.float32)
        qf[q] = lanes.reshape(TOK * 8, HD)
        for h in range(8):
            rows = qf[q, pl.ds(h, TOK, stride=8), :]
            qsend[h // 2, h % 2, q * TOK : (q + 1) * TOK, :] = rows.astype(jnp.bfloat16)
    loads[1].wait()
    turn_blocks = []
    for b in range(TOK // BLK):
        parts = []
        for r in range(BLK):
            row = kv_v[b * BLK + r].astype(jnp.float32)
            parts += [row[:, :HD], row[:, HD:]]
        turn_blocks.append(jnp.concatenate(parts, axis=0))
    mixed = split(turn_blocks)
    for t in range(NX):
        for b in range(TOK // BLK):
            kvsend[t, b] = mixed[t * 16 : (t + 1) * 16, b * HD : (b + 1) * HD]

    pl.semaphore_wait(barrier, NZ * NY * NC * NX - 1)

    def turn_copies(d):
        to = lax.rem(x + d, NX)
        return (
            pltpu.make_async_remote_copy(
                qsend.at[to], qarr.at[x], turn_send.at[0, d - 1], turn_recv.at[0, d - 1],
                device_id=(store, to), device_id_type=MESH,
            ),
            pltpu.make_async_remote_copy(
                kvsend.at[to], kvarr.at[x], turn_send.at[1, d - 1], turn_recv.at[1, d - 1],
                device_id=(store, to), device_id_type=MESH,
            ),
        )

    for d in range(1, NX):
        for copy in turn_copies(d):
            copy.start()
    qarr[x] = qsend[x]
    kvarr[x] = kvsend[x]

    loads[2].wait()
    loads[3].wait()

    def send_session(k, _):
        j, i = k // NZ, k % NZ
        half = i // 2 + 1
        dz = jnp.where(i == NZ - 1, 0, jnp.where(i % 2 == 0, half, NZ - half))
        z2, y2 = lax.rem(z + dz, NZ), lax.rem(y + j // NC, NY)
        core2 = lax.rem(core + j % NC, NC)
        session = (z2 * NY + y2) * NC + core2
        tiles = []
        for c in range(CAP):
            slot = slot_ref[session * CAP + c]
            scale = scale_ref[slot].astype(jnp.float32)
            anchor = anchor_v[slot].astype(jnp.float32)
            parts = []
            for r in range(BLK):
                delta = delta_v[slot, r].astype(jnp.float32)
                parts.append(anchor[:, :HD] + scale[:, 0:1] * delta[:, :HD])
                parts.append(anchor[:, HD:] + scale[:, 1:2] * delta[:, HD:])
            tiles.append(jnp.concatenate(parts, axis=0))
        mixed = split(tiles)
        for t in range(NX):
            for c in range(CAP):
                send[k, t, c] = mixed[t * 16 : (t + 1) * 16, c * HD : (c + 1) * HD]
        mine = (core * 1 + y * NC) * PER_STEP + z * NX + x
        for d in range(NX):
            to = lax.rem(x + d, NX)
            copy = pltpu.make_async_remote_copy(
                send.at[k, to], arr.at[mine], send_sem.at[j], recv_sem.at[j],
                device_id=(session, to), device_id_type=MESH,
            )
            if d:
                copy.start()
            else:
                pl.when(k != NZ - 1)(copy.start)

        @pl.when(k == NZ - 1)
        def _():
            arr[mine] = send[NZ - 1, x]

        return 0

    lax.fori_loop(0, PLANES * NZ, send_session, 0)

    for d in range(1, NX):
        for copy in turn_copies(d):
            copy.wait()

    ones = jnp.ones((KEYS, HD), jnp.bfloat16)
    values[0, :, HD:] = ones
    values[1, :, HD:] = ones

    def unpack(tiles, count):
        flat[pl.ds(0, count * 4), :] = tiles.astype(jnp.float32).reshape(count * 4, HD)
        for h in range(HEADS):
            keys[h, pl.ds(0, count), :] = flat[pl.ds(h, count, stride=4), :].astype(jnp.bfloat16)
            values[h, pl.ds(0, count), :HD] = flat[pl.ds(2 + h, count, stride=4), :].astype(
                jnp.bfloat16
            )

    unpack(kvarr[...].reshape(TURN_TILES, 16, HD), TURN)
    token = lax.broadcasted_iota(jnp.int32, (ROWS, TURN), 0) & (TOK - 1)
    position = lax.broadcasted_iota(jnp.int32, (ROWS, TURN), 1)
    for h in range(HEADS):
        for g in range(NX):
            scores = lax.dot_general(
                qarr[g, h], keys[h, :TURN, :], (((1,), (1,)), ((), ())),
                preferred_element_type=jnp.float32,
            )
            scores = jnp.where(position <= token + g * TOK, scores * SCALE2, LOW)
            peak = jnp.max(scores, axis=1, keepdims=True)
            power = jnp.exp2(scores - peak).astype(jnp.bfloat16)
            acc[h, g] = jnp.dot(power, values[h, :TURN, :], preferred_element_type=jnp.float32)
            top[h, g] = jnp.broadcast_to(peak, (ROWS, HD))

    def attend(j, _):
        source = lax.rem(y + NY - j // NC, NY) * NC + lax.rem(core + NC - j % NC, NC)
        first = source * PER_STEP

        def arrived(count):
            span = arr.at[pl.ds(first, count)]
            pltpu.make_async_remote_copy(
                span, span, send_sem.at[j], recv_sem.at[j],
                device_id=(store, lax.rem(x + 1, NX)), device_id_type=MESH,
            ).wait_recv()

        @pl.when(j == 0)
        def _():
            arrived(PER_STEP - 1)

        @pl.when(j != 0)
        def _():
            arrived(PER_STEP)

        unpack(arr[pl.ds(first, PER_STEP)].reshape(PER_STEP * CAP, 16, HD), KEYS)
        bias = bias_ref[source]
        for h in range(HEADS):
            for g in range(NX):
                scores = lax.dot_general(
                    qarr[g, h], keys[h], (((1,), (1,)), ((), ())),
                    preferred_element_type=jnp.float32,
                )
                scores = scores * SCALE2 + bias
                before = top[h, g][:, 0:1]
                peak = jnp.maximum(before, jnp.max(scores, axis=1, keepdims=True))
                power = jnp.exp2(scores - peak).astype(jnp.bfloat16)
                acc[h, g] = acc[h, g] * jnp.exp2(before - peak) + jnp.dot(
                    power, values[h], preferred_element_type=jnp.float32
                )
                top[h, g] = jnp.broadcast_to(peak, (ROWS, HD))
        return 0

    lax.fori_loop(0, PLANES, attend, 0)

    def back_copy(d):
        to = lax.rem(x + d, NX)
        return pltpu.make_async_remote_copy(
            outsend.at[to], outarr.at[x], back_send.at[d - 1], back_recv.at[d - 1],
            device_id=(store, to), device_id_type=MESH,
        )

    for d in (2, 1, 3, 0):
        g = lax.rem(x + d, NX)
        for h in range(HEADS):
            total = acc[h, g]
            outsend[g, h] = (total[:, :HD] / total[:, HD:]).astype(jnp.bfloat16)
        if d:
            back_copy(d).start()
        else:
            outarr[x] = outsend[x]

    def place(b, _):
        stage[b] = arr[inv_ref[b] // CAP, inv_ref[b] % CAP]
        return 0

    lax.fori_loop(0, NBLK, place, 0, unroll=8)
    stage[NBLK:] = kvarr[...].reshape(TURN_TILES, 16, HD)
    cache_copy = pltpu.make_async_copy(stage, cache_hbm, store_sem.at[0])
    cache_copy.start()

    for d in range(1, NX):
        back_copy(d).wait()
    for t in range(NX):
        for hh in range(HEADS):
            for q in range(QPG):
                qf[q, pl.ds(t * 2 + hh, TOK, stride=8), :] = outarr[
                    t, hh, q * TOK : (q + 1) * TOK, :
                ].astype(jnp.float32)
    for q in range(QPG):
        att_v[:, :, q * HD : (q + 1) * HD] = qf[q].reshape(TOK, 8, HD).astype(jnp.bfloat16)
    att_copy = pltpu.make_async_copy(att_v, att_hbm, store_sem.at[1])
    att_copy.start()

    for j in range(PLANES):
        count = PER_STEP - 1 if j == 0 else PER_STEP
        span = arr.at[pl.ds(j * PER_STEP, count)]
        pltpu.make_async_remote_copy(
            span, span, send_sem.at[j], recv_sem.at[j],
            device_id=(store, lax.rem(x + 1, NX)), device_id_type=MESH,
        ).wait_send()
    cache_copy.wait()
    att_copy.wait()


def shards(slot_anchor, slot_delta, slot_scale, send_slot, recv_block, turn_queries, turn_kv):
    slots = jnp.maximum(send_slot, 0).reshape(-1)
    planned = recv_block[0].reshape(NZ, PLANES, NX, CAP).transpose(1, 0, 2, 3)
    bias = jnp.where(planned >= 0, 0.0, LOW).astype(jnp.float32)
    bias = jnp.repeat(bias.reshape(PLANES, 1, PER_STEP * CAP), BLK, axis=2)
    places = planned.reshape(-1, 1)
    hits = places == jnp.arange(NBLK)[None, :]
    inverse = jnp.sum(jnp.where(hits, jnp.arange(NBLK + 256)[:, None], 0), axis=0)
    bf16, f32 = jnp.bfloat16, jnp.float32
    cache, attended = pl.pallas_call(
        body,
        out_shape=(
            jax.ShapeDtypeStruct((NBLK + TURN_TILES, 16, HD), bf16),
            jax.ShapeDtypeStruct((TOK, 8, QPG * HD), bf16),
        ),
        in_specs=[
            pl.BlockSpec(memory_space=pl.ANY),
            pl.BlockSpec(memory_space=pl.ANY),
            pl.BlockSpec(memory_space=pltpu.VMEM),
            pl.BlockSpec(memory_space=pltpu.SMEM),
            pl.BlockSpec(memory_space=pltpu.SMEM),
            pl.BlockSpec(memory_space=pltpu.VMEM),
            pl.BlockSpec(memory_space=pl.ANY),
            pl.BlockSpec(memory_space=pl.ANY),
        ],
        out_specs=(pl.BlockSpec(memory_space=pl.ANY), pl.BlockSpec(memory_space=pl.ANY)),
        scratch_shapes=[
            pltpu.VMEM(slot_anchor.shape, bf16),
            pltpu.VMEM(slot_delta.shape, bf16),
            pltpu.VMEM(turn_queries.shape, bf16),
            pltpu.VMEM(turn_kv.shape, bf16),
            pltpu.VMEM(turn_queries.shape, bf16),
            pltpu.VMEM((64, 64), bf16),
            pltpu.VMEM((QPG, TOK * 8, HD), f32),
            pltpu.VMEM((NX, HEADS, ROWS, HD), bf16),
            pltpu.VMEM((NX, HEADS, ROWS, HD), bf16),
            pltpu.VMEM((NX, TOK // BLK, 16, HD), bf16),
            pltpu.VMEM((NX, TOK // BLK, 16, HD), bf16),
            pltpu.VMEM((PLANES * NZ, NX, CAP, 16, HD), bf16),
            pltpu.VMEM((PLANES * PER_STEP, CAP, 16, HD), bf16),
            pltpu.VMEM((KEYS * 4, HD), f32),
            pltpu.VMEM((HEADS, KEYS, HD), bf16),
            pltpu.VMEM((HEADS, KEYS, 2 * HD), bf16),
            pltpu.VMEM((HEADS, NX, ROWS, 2 * HD), f32),
            pltpu.VMEM((HEADS, NX, ROWS, HD), f32),
            pltpu.VMEM((NX, HEADS, ROWS, HD), bf16),
            pltpu.VMEM((NX, HEADS, ROWS, HD), bf16),
            pltpu.VMEM((NBLK + TURN_TILES, 16, HD), bf16),
            pltpu.SemaphoreType.DMA((4,)),
            pltpu.SemaphoreType.DMA((PLANES,)),
            pltpu.SemaphoreType.DMA((PLANES,)),
            pltpu.SemaphoreType.DMA((2, NX - 1)),
            pltpu.SemaphoreType.DMA((2, NX - 1)),
            pltpu.SemaphoreType.DMA((NX - 1,)),
            pltpu.SemaphoreType.DMA((NX - 1,)),
            pltpu.SemaphoreType.DMA((2,)),
        ],
        compiler_params=pltpu.CompilerParams(
            collective_id=0, has_side_effects=True, vmem_limit_bytes=48 * 2**20
        ),
        name="restore_attend",
    )(
        slot_anchor, slot_delta, slot_scale, slots, inverse, bias, turn_queries, turn_kv
    )
    cache = cache.reshape(NBLK + TURN_TILES, BLK, 2, HEADS, HD).transpose(0, 1, 3, 2, 4)
    return cache.reshape(1, (NBLK + TURN_TILES) * BLK, HEADS, 2 * HD), attended


def solution(mesh):
    placed = (
        P(("store", "tp"), None, None),
        P(("store", "tp"), None, None, None),
        P(("store", "tp"), None, None),
        P(("store", "tp"), None, None),
        P("store", None, None),
        P(("store", "tp"), None, None),
        P(("store", "tp"), None, None),
    )
    return jax.shard_map(
        shards,
        mesh=mesh,
        in_specs=placed,
        out_specs=(P("store", None, "tp", None), P(("store", "tp"), None, None)),
        check_vma=False,
    )
```

time: 481 us -> 165 us (0.34)
  the two profiles are of different devices: /device:TPU:58 before, /device:TPU:1 now
where the time goes in v1:
time: 165 us; the launch traced here: 164 us
  Pallas kernels  147 us (89%)
  local copies, waits for them, and re-layouts  14.8 us (9%)
  other arithmetic  2.01 us (1%)
    pallas_call x1, Pallas kernels, shards(): pl.pallas_call(body, out_shape=(jax.ShapeDtypeStruct((NBLK + TURN_TILES,...  147 us
    unnamed x9, local copies, waits for them, and re-layouts  13.1 us

profile of v1, /device:TPU:1, one launch (start us, length us, event | category | flops | bytes accessed | tf_op | source)
XLA Modules:
  0.0 164.1 jit_solution(9197175948481619055)
XLA Ops:
  0.6 0.7 broadcast_maximum_fusion
  1.3 0.7 reduce
  2.0 0.1 copy.18
  2.1 0.1 reshape.24.slot_ref
  2.3 0.2 reshape_squeeze.3
  2.4 0.5 copy.19
  2.9 0.2 eq.15
  3.2 0.6 select_reduce_fusion.inv_ref
  3.8 0.4 copy.25
  4.3 0.1 broadcast_in_dim.31
  4.3 0.1 copy.23.bias_ref
  4.5 1.2 copy.22.scale_ref
  5.7 0.0 copy-start
  5.7 1.3 copy-done
  7.0 0.0 copy-start.1
  7.0 1.0 copy-done.1
  8.0 0.0 copy-start.2
  8.0 0.9 copy-done.2
  8.9 146.6 %restore_attend.1 = (bf16[1056,16,128]{2,1,0:T(8,128)(2,1)}, bf16[32,8,1024]{2,1,0:T(8,128)(2,1)S(1)}) custom-call(bf16[320,8,256]{2,1,0:T(8,128)(2,1)S(1)} %copy-done, bf16[320,4,8,256]{3,2,1,0:T(8,128)(2,1)} %delta_hbm.1, bf16[320,8,2]{2,1,0:T(8,128)(2,1)S(1)} %copy.22.scale_ref, s32[320]{0:T(512)S(1)} %reshape.24.slot_ref, ...), custom_call_target="tpu_custom_call" | custom-call | tf_op jit(solution)/shard_map/restore_attend/pallas_call | solution.py:285
  155.5 7.8 %copy.29 = bf16[1,4224,2,256]{3,2,1,0:T(2,128)(2,1)} copy(bf16[1,4224,2,256]{3,2,1,0:T(2,128)(2,1)} %bitcast.12) | data formatting | bytes 8650752
  163.3 0.8 copy.30
  (2 shorter events, 0.1 us)
Async XLA Ops:
  5.7 1.3 copy-start
  7.0 1.0 copy-start.1
  8.0 0.9 copy-start.2

commit v2 on v1

v2 whole, which is shorter than its diff:
```python
import math

import jax
import jax.numpy as jnp
from jax import lax
from jax.experimental import pallas as pl
from jax.experimental.pallas import tpu as pltpu
from jax.sharding import PartitionSpec as P

MESH = pl.DeviceIdType.MESH
NZ, NY, NC, NX = 8, 4, 2, 4
PLANES = NY * NC
PER_STEP = NZ * NX
CAP = 5
BLK = 4
HD = 128
QPG = 8
NBLK = 1024
TOK = 32
TURN = TOK * NX
HEADS = 2
ROWS = QPG * TOK
KEYS = PER_STEP * CAP * BLK
TURN_TILES = TURN // BLK
SCALE2 = math.log2(math.e) / math.sqrt(HD)
LOW = -1e30
Y_STEPS = sum(d << (2 * i) for i, d in enumerate((2, 2, 1, 3, 1, 3, 0, 0)))
C_STEPS = sum(d << i for i, d in enumerate((0, 1, 0, 1, 1, 0, 1, 0)))
Z_ORDER = (4, 3, 5, 0, 2, 6, 1, 7)
Z_STEPS = sum(d << (3 * i) for i, d in enumerate(Z_ORDER))
SELF = (PLANES - 1) * NZ + Z_ORDER.index(0)
PIECES = 8
VMEM = 62148608


def body(
    anchor_hbm, delta_hbm, scale_hbm, slot_hbm, recv_hbm, q_hbm, kv_hbm,
    cache_out, att_v,
    anchor_v, delta_v, scale_v, slot_ref, recv_ref, q_v, kv_v, stage, spread, bias_v, inv_v, inv_ref,
    perm, qf, qsend, qarr, kvsend, kvarr, send, arr,
    flat, keys, values, acc, top, outsend, outarr,
    load_sem, send_sem, recv_sem, turn_send, turn_recv, back_send, back_recv, inv_sem, out_sem,
):
    store = lax.axis_index("store")
    x = lax.axis_index("tp")
    z, y, core = store // (NY * NC), (store // NC) % NY, store % NC

    loads = [
        pltpu.make_async_copy(src, dst, load_sem.at[i])
        for i, (src, dst) in enumerate(
            (
                (q_hbm, q_v), (kv_hbm, kv_v), (scale_hbm, scale_v), (slot_hbm, slot_ref),
                (recv_hbm, recv_ref), (anchor_hbm, anchor_v), (delta_hbm, delta_v),
            )
        )
    ]
    for load in loads:
        load.start()

    barrier = pltpu.get_barrier_semaphore()

    me = store * NX + x
    devices = NZ * NY * NC * NX

    def greet(i, _):
        other = (me + 1 + i) & (devices - 1)
        pl.semaphore_signal(
            barrier, inc=1, device_id=(other >> 2, other & 3), device_id_type=MESH
        )
        return 0

    lax.fori_loop(0, devices - 1, greet, 0, unroll=15)

    out_row = lax.broadcasted_iota(jnp.int32, (64, 64), 0)
    in_row = lax.broadcasted_iota(jnp.int32, (64, 64), 1)
    wanted = ((out_row >> 1) & 7) * 8 + (out_row >> 4) * 2 + (out_row & 1)
    perm[...] = jnp.where(in_row == wanted, 1.0, 0.0).astype(jnp.bfloat16)

    def split(tiles):
        wide = jnp.concatenate(tiles, axis=1).astype(jnp.bfloat16)
        return jnp.dot(perm[...], wide, preferred_element_type=jnp.float32).astype(jnp.bfloat16)

    loads[2].wait()
    scale = scale_v[...].astype(jnp.float32)
    slots = scale.shape[2]
    for kv in range(2):
        flat[kv * 8 : kv * 8 + 8, :] = scale[:, kv, :HD]
        flat[16 + kv * 8 : 24 + kv * 8, :] = scale[:, kv, HD : 2 * HD]
        flat[32 + kv * 8 : 40 + kv * 8, : slots - 2 * HD] = scale[:, kv, 2 * HD :]
    for slot in range(slots):
        part, lane = slot // HD * 16, slot % HD
        for kv in range(2):
            column = flat[part + kv * 8 : part + kv * 8 + 8, lane : lane + 1]
            spread[kv, slot] = jnp.broadcast_to(column, (8, HD))

    loads[0].wait()
    for q in range(QPG):
        lanes = q_v[:, :, q * HD : (q + 1) * HD].astype(jnp.float32)
        qf[q] = lanes.reshape(TOK * 8, HD)
        for h in range(8):
            rows = qf[q, pl.ds(h, TOK, stride=8), :]
            qsend[h // 2, h % 2, q * TOK : (q + 1) * TOK, :] = rows.astype(jnp.bfloat16)
    loads[1].wait()
    turn_blocks = []
    for b in range(TOK // BLK):
        parts = []
        for r in range(BLK):
            row = kv_v[b * BLK + r].astype(jnp.float32)
            parts += [row[:, :HD], row[:, HD:]]
        turn_blocks.append(jnp.concatenate(parts, axis=0))
    mixed = split(turn_blocks)
    for t in range(NX):
        for b in range(TOK // BLK):
            kvsend[t, b] = mixed[t * 16 : (t + 1) * 16, b * HD : (b + 1) * HD]

    pl.semaphore_wait(barrier, devices - 1)

    def turn_copies(d):
        to = lax.rem(x + d, NX)
        return (
            pltpu.make_async_remote_copy(
                qsend.at[to], qarr.at[x], turn_send.at[0, d - 1], turn_recv.at[0, d - 1],
                device_id=(store, to), device_id_type=MESH,
            ),
            pltpu.make_async_remote_copy(
                kvsend.at[to], kvarr.at[x], turn_send.at[1, d - 1], turn_recv.at[1, d - 1],
                device_id=(store, to), device_id_type=MESH,
            ),
        )

    for load in loads[3:]:
        load.wait()

    def offsets(j):
        return (Y_STEPS >> (2 * j)) & (NY - 1), (C_STEPS >> j) & (NC - 1)

    def z_offset(i):
        return (Z_STEPS >> (3 * i)) & (NZ - 1)

    def send_session(k, _):
        j, i = k >> 3, k & 7
        dy, dc = offsets(j)
        z2, y2, core2 = (z + z_offset(i)) & (NZ - 1), (y + dy) & (NY - 1), (core + dc) & (NC - 1)
        session = (z2 * NY + y2) * NC + core2
        box = j + jnp.where(k >= (PLANES - 1) * NZ + NZ // 2, 1, 0)
        tiles = []
        for c in range(CAP):
            slot = jnp.maximum(slot_ref[c, 0, session], 0)
            key_scale, value_scale = spread[0, slot], spread[1, slot]
            anchor = anchor_v[slot].astype(jnp.float32)
            parts = []
            for r in range(BLK):
                delta = delta_v[slot, r].astype(jnp.float32)
                parts.append(anchor[:, :HD] + key_scale * delta[:, :HD])
                parts.append(anchor[:, HD:] + value_scale * delta[:, HD:])
            tiles.append(jnp.concatenate(parts, axis=0))
        mixed = split(tiles)
        for t in range(NX):
            for c in range(CAP):
                send[k, t, c] = mixed[t * 16 : (t + 1) * 16, c * HD : (c + 1) * HD]
        mine = (y * NC + core) * PER_STEP + z * NX + x
        for d in range(NX):
            to = (x + d) & (NX - 1)
            copy = pltpu.make_async_remote_copy(
                send.at[k, to], arr.at[mine], send_sem.at[j], recv_sem.at[box],
                device_id=(session, to), device_id_type=MESH,
            )
            if d:
                copy.start()
            else:
                pl.when(k != SELF)(copy.start)

        @pl.when(k == SELF)
        def _():
            arr[mine] = send[SELF, x]

        return 0

    lax.fori_loop(0, NZ, send_session, 0)
    for d in range(1, NX):
        for copy in turn_copies(d):
            copy.start()
    qarr[x] = qsend[x]
    kvarr[x] = kvsend[x]
    lax.fori_loop(NZ, PLANES * NZ, send_session, 0)

    recv_rows = [recv_ref[c] for c in range(CAP)]
    dead = [jnp.where(row >= 0, 0.0, 1.0) for row in recv_rows]
    dead = jnp.concatenate(dead + [jnp.zeros((8 - CAP, PER_STEP * PLANES), jnp.float32)], axis=0)
    dead = dead.astype(jnp.bfloat16)
    holder = lax.broadcasted_iota(jnp.int32, (PER_STEP * PLANES, HD), 0)
    lane = lax.broadcasted_iota(jnp.int32, (PER_STEP * PLANES, HD), 1)
    line = jnp.zeros_like(lane)
    for i, dz in enumerate(Z_ORDER):
        line = jnp.where((lane >> 4) == i, ((z - dz) & (NZ - 1)) * PER_STEP, line)
    line = line + ((lane >> 2) & 3)

    def origin(j):
        dy, dc = offsets(j)
        return ((y - dy) & (NY - 1)) * NC + ((core - dc) & (NC - 1))

    def mark(j, _):
        pick = jnp.where(holder == line + origin(j) * NX, 1.0, 0.0).astype(jnp.bfloat16)
        bias_v[j] = jnp.dot(dead, pick, preferred_element_type=jnp.float32) * LOW
        return 0

    lax.fori_loop(0, PLANES, mark, 0)

    columns = jnp.concatenate(
        recv_rows + [jnp.full((8 - CAP, PER_STEP * PLANES), -1, jnp.int32)], axis=0
    ).T
    holder = lax.broadcasted_iota(jnp.int32, (PER_STEP * PLANES, 1), 0)
    place_of = (((holder >> 2) & 7) * PER_STEP + (holder >> 5) * NX + (holder & 3)) * 8
    for part in range(NBLK // HD):
        block = lax.broadcasted_iota(jnp.int32, (PER_STEP * PLANES, HD), 1) + part * HD
        found = jnp.zeros((PER_STEP * PLANES, HD), jnp.int32)
        for c in range(CAP):
            found = jnp.maximum(found, jnp.where(columns[:, c : c + 1] == block, place_of + c, 0))
        inv_v[part : part + 1, :] = jnp.max(found, axis=0, keepdims=True)
    inv_copy = pltpu.make_async_copy(inv_v, inv_ref, inv_sem)
    inv_copy.start()

    for d in range(1, NX):
        for copy in turn_copies(d):
            copy.wait()

    ones = jnp.ones((KEYS, HD), jnp.bfloat16)
    values[0, :, HD:] = ones
    values[1, :, HD:] = ones

    def unpack(count):
        for h in range(HEADS):
            keys[h, pl.ds(0, count), :] = flat[pl.ds(h, count, stride=4), :].astype(jnp.bfloat16)
            values[h, pl.ds(0, count), :HD] = flat[pl.ds(2 + h, count, stride=4), :].astype(
                jnp.bfloat16
            )

    flat[: TURN * 4, :] = kvarr[...].reshape(TURN * 4, HD).astype(jnp.float32)
    unpack(TURN)
    token = lax.broadcasted_iota(jnp.int32, (ROWS, TURN), 0) & (TOK - 1)
    position = lax.broadcasted_iota(jnp.int32, (ROWS, TURN), 1)
    for h in range(HEADS):
        for g in range(NX):
            scores = lax.dot_general(
                qarr[g, h], keys[h, :TURN, :], (((1,), (1,)), ((), ())),
                preferred_element_type=jnp.float32,
            )
            scores = jnp.where(position <= token + g * TOK, scores * SCALE2, LOW)
            peak = jnp.max(scores, axis=1, keepdims=True)
            power = jnp.exp2(scores - peak).astype(jnp.bfloat16)
            acc[h, g] = jnp.dot(power, values[h, :TURN, :], preferred_element_type=jnp.float32)
            top[h, g] = jnp.broadcast_to(peak, (ROWS, HD))

    def receive(j, box, count, z_from, z_to):
        first = origin(j) * PER_STEP
        span = arr.at[pl.ds(0, count)]
        pltpu.make_async_remote_copy(
            span, span, send_sem.at[0], recv_sem.at[box],
            device_id=(store, (x + 1) & (NX - 1)), device_id_type=MESH,
        ).wait_recv()
        lines = (z_to - z_from) * NX
        for i in range(z_from, z_to):
            at = first + ((z - Z_ORDER[i]) & (NZ - 1)) * NX
            for c in range(CAP):
                tiles = arr[pl.ds(at, NX), c].reshape(NX * 16, HD).astype(jnp.float32)
                flat[pl.ds((c * lines + (i - z_from) * NX) * 16, NX * 16), :] = tiles
        unpack(lines * CAP * BLK)
        rows = bias_v[j]
        return jnp.concatenate(
            [rows[c : c + 1, z_from * 16 : z_to * 16] for c in range(CAP)], axis=1
        )

    def update(bias, h, g):
        scores = lax.dot_general(
            qarr[g, h], keys[h, : bias.shape[1]], (((1,), (1,)), ((), ())),
            preferred_element_type=jnp.float32,
        )
        scores = scores * SCALE2 + bias
        before = top[h, g][:, 0:1]
        peak = jnp.maximum(before, jnp.max(scores, axis=1, keepdims=True))
        power = jnp.exp2(scores - peak).astype(jnp.bfloat16)
        total = acc[h, g] * jnp.exp2(before - peak) + jnp.dot(
            power, values[h, : bias.shape[1]], preferred_element_type=jnp.float32
        )
        return total, peak

    def attend(bias):
        for h in range(HEADS):
            for g in range(NX):
                acc[h, g], peak = update(bias, h, g)
                top[h, g] = jnp.broadcast_to(peak, (ROWS, HD))

    def step(j, _):
        attend(receive(j, j, PER_STEP, 0, NZ))
        return 0

    lax.fori_loop(0, PLANES - 1, step, 0)
    last, half = PLANES - 1, NZ // 2
    attend(receive(last, last, PER_STEP // 2 - 1, 0, half))
    bias = receive(last, last + 1, PER_STEP // 2, half, NZ)
    def back_copy(d):
        to = lax.rem(x + d, NX)
        return pltpu.make_async_remote_copy(
            outsend.at[to], outarr.at[x], back_send.at[d - 1], back_recv.at[d - 1],
            device_id=(store, to), device_id_type=MESH,
        )

    for d in (2, 1, 3, 0):
        g = lax.rem(x + d, NX)
        for h in range(HEADS):
            total, _ = update(bias, h, g)
            outsend[g, h] = (total[:, :HD] / total[:, HD:]).astype(jnp.bfloat16)
        if d:
            back_copy(d).start()
        else:
            outarr[x] = outsend[x]

    inv_copy.wait()

    def place(b, _):
        found = inv_ref[b >> 7, b & (HD - 1)]
        source = jnp.clip(found >> 3, 0, PLANES * PER_STEP - 1)
        stage[b] = arr[source, jnp.minimum(found & 7, CAP - 1)]
        return 0

    many = (NBLK + TURN_TILES) // PIECES
    moves = [
        pltpu.make_async_copy(
            stage.at[pl.ds(p * many, many)], cache_out.at[pl.ds(p * many, many)], out_sem.at[p]
        )
        for p in range(PIECES)
    ]
    stage[NBLK:] = kvarr[...].reshape(TURN_TILES, 16, HD)
    for p in range(PIECES):
        end = min((p + 1) * many, NBLK)
        lax.fori_loop(p * many, end, place, 0, unroll=8)
        moves[p].start()

    for d in range(1, NX):
        back_copy(d).wait()
    for t in range(NX):
        for hh in range(HEADS):
            for q in range(QPG):
                qf[q, pl.ds(t * 2 + hh, TOK, stride=8), :] = outarr[
                    t, hh, q * TOK : (q + 1) * TOK, :
                ].astype(jnp.float32)
    for q in range(QPG):
        att_v[:, :, q * HD : (q + 1) * HD] = qf[q].reshape(TOK, 8, HD).astype(jnp.bfloat16)

    for move in moves:
        move.wait()
    for j in range(PLANES):
        count = PER_STEP - 1 if j == last else PER_STEP
        span = arr.at[pl.ds(0, count)]
        pltpu.make_async_remote_copy(
            span, span, send_sem.at[j], recv_sem.at[j],
            device_id=(store, (x + 1) & (NX - 1)), device_id_type=MESH,
        ).wait_send()


def write_out(cache_in, att_in, cache_hbm, att_hbm, sems):
    copies = (
        pltpu.make_async_copy(cache_in, cache_hbm, sems.at[0]),
        pltpu.make_async_copy(att_in, att_hbm, sems.at[1]),
    )
    for copy in copies:
        copy.start()
    for copy in copies:
        copy.wait()


def shards(slot_anchor, slot_delta, slot_scale, send_slot, recv_block, turn_queries, turn_kv):
    bf16, f32 = jnp.bfloat16, jnp.float32
    slots = slot_anchor.shape[0]
    scales = slot_scale.transpose(1, 2, 0)
    cache_shape = (NBLK + TURN_TILES, 16, HD)
    in_hbm = pl.BlockSpec(memory_space=pltpu.HBM)
    in_vmem = pl.BlockSpec(memory_space=pltpu.VMEM)
    cache, attended = pl.pallas_call(
        body,
        out_shape=(
            pltpu.VMEM(cache_shape, bf16),
            pltpu.VMEM(turn_queries.shape, bf16),
        ),
        in_specs=[
            in_hbm, in_hbm, in_hbm, in_hbm, in_hbm, in_hbm, in_hbm,
        ],
        out_specs=(pl.BlockSpec(memory_space=pltpu.VMEM), pl.BlockSpec(memory_space=pltpu.VMEM)),
        scratch_shapes=[
            pltpu.VMEM(slot_anchor.shape, bf16),
            pltpu.VMEM(slot_delta.shape, bf16),
            pltpu.VMEM(scales.shape, bf16),
            pltpu.SMEM((CAP, 1, PLANES * NZ), jnp.int32),
            pltpu.VMEM((CAP, 1, PLANES * PER_STEP), jnp.int32),
            pltpu.VMEM(turn_queries.shape, bf16),
            pltpu.VMEM(turn_kv.shape, bf16),
            pltpu.VMEM(cache_shape, bf16),
            pltpu.VMEM((2, slots, 8, HD), f32),
            pltpu.VMEM((PLANES, 8, HD), f32),
            pltpu.VMEM((8, HD), jnp.int32),
            pltpu.SMEM((8, HD), jnp.int32),
            pltpu.VMEM((64, 64), bf16),
            pltpu.VMEM((QPG, TOK * 8, HD), f32),
            pltpu.VMEM((NX, HEADS, ROWS, HD), bf16),
            pltpu.VMEM((NX, HEADS, ROWS, HD), bf16),
            pltpu.VMEM((NX, TOK // BLK, 16, HD), bf16),
            pltpu.VMEM((NX, TOK // BLK, 16, HD), bf16),
            pltpu.VMEM((PLANES * NZ, NX, CAP, 16, HD), bf16),
            pltpu.VMEM((PLANES * PER_STEP, CAP, 16, HD), bf16),
            pltpu.VMEM((KEYS * 4, HD), f32),
            pltpu.VMEM((HEADS, KEYS, HD), bf16),
            pltpu.VMEM((HEADS, KEYS, 2 * HD), bf16),
            pltpu.VMEM((HEADS, NX, ROWS, 2 * HD), f32),
            pltpu.VMEM((HEADS, NX, ROWS, HD), f32),
            pltpu.VMEM((NX, HEADS, ROWS, HD), bf16),
            pltpu.VMEM((NX, HEADS, ROWS, HD), bf16),
            pltpu.SemaphoreType.DMA((7,)),
            pltpu.SemaphoreType.DMA((PLANES,)),
            pltpu.SemaphoreType.DMA((PLANES + 1,)),
            pltpu.SemaphoreType.DMA((2, NX - 1)),
            pltpu.SemaphoreType.DMA((2, NX - 1)),
            pltpu.SemaphoreType.DMA((NX - 1,)),
            pltpu.SemaphoreType.DMA((NX - 1,)),
            pltpu.SemaphoreType.DMA,
            pltpu.SemaphoreType.DMA((PIECES,)),
        ],
        compiler_params=pltpu.CompilerParams(
            collective_id=0, has_side_effects=True, vmem_limit_bytes=VMEM
        ),
        name="restore_attend",
    )(
        slot_anchor, slot_delta, scales, send_slot.transpose(2, 0, 1),
        recv_block.transpose(2, 0, 1), turn_queries, turn_kv,
    )
    cache, attended = pl.pallas_call(
        write_out,
        out_shape=(
            jax.ShapeDtypeStruct(cache_shape, bf16),
            jax.ShapeDtypeStruct(turn_queries.shape, bf16),
        ),
        in_specs=[in_vmem, in_vmem],
        out_specs=(in_hbm, in_hbm),
        scratch_shapes=[pltpu.SemaphoreType.DMA((2,))],
        compiler_params=pltpu.CompilerParams(vmem_limit_bytes=2**20),
        name="write_out",
    )(cache, attended)
    cache = cache.reshape(NBLK + TURN_TILES, BLK, 2, HEADS, HD).transpose(0, 1, 3, 2, 4)
    return cache.reshape(1, (NBLK + TURN_TILES) * BLK, HEADS, 2 * HD), attended


def solution(mesh):
    placed = (
        P(("store", "tp"), None, None),
        P(("store", "tp"), None, None, None),
        P(("store", "tp"), None, None),
        P(("store", "tp"), None, None),
        P("store", None, None),
        P(("store", "tp"), None, None),
        P(("store", "tp"), None, None),
    )
    return jax.shard_map(
        shards,
        mesh=mesh,
        in_specs=placed,
        out_specs=(P("store", None, "tp", None), P(("store", "tp"), None, None)),
        check_vma=False,
    )
```

time: 165 us -> 143 us (0.87)
  local copies, waits for them, and re-layouts: 14.8 us -> 0 us
  Pallas kernels: 147 us -> 142 us
  other arithmetic: 2.01 us -> 0 us
    unnamed x9 -> x0, local copies, waits for them, and re-layouts: 13.1 us -> none
    pallas_call x1 -> x2, Pallas kernels: 147 us -> 142 us  [the longest x1 140 us: shards(): pl.pallas_call(body, out_shape=(pltpu.VMEM(cache_shape, bf16), pltpu.VMEM...]
where the time goes in v2:
time: 143 us
  Pallas kernels  142 us (99%)
    pallas_call x1, Pallas kernels, shards(): pl.pallas_call(body, out_shape=(pltpu.VMEM(cache_shape, bf16), pltpu.VMEM...  140 us

profile of v2, /device:TPU:1, one launch (start us, length us, event | category | flops | bytes accessed | tf_op | source)
XLA Modules:
  0.0 143.0 jit_solution(7066135356872850629)
XLA Ops:
  0.6 140.1 %restore_attend.1 = (bf16[1056,16,128]{2,1,0:T(8,128)(2,1)S(1)}, bf16[32,8,1024]{2,1,0:T(8,128)(2,1)S(1)}) custom-call(bf16[320,8,256]{2,1,0:T(8,128)(2,1)} %anchor_hbm.1, bf16[320,4,8,256]{3,2,1,0:T(8,128)(2,1)} %delta_hbm.1, bf16[8,2,320]{2,1,0:T(2,128)(2,1)} %bitcast.8, s32[5,1,64]{2,1,0:T(1,128)} %bitcast.10, s32[5,1,256]{2,1,0:T(1,128)} %bitcast.9, ...), custom_call_target="tpu_custom_call" | custom-call | tf_op jit(solution)/shard_map/restore_attend/pallas_call | solution.py:379
  140.7 2.2 %write_out.1 = (bf16[1056,16,128]{2,1,0:T(8,128)(2,1)}, bf16[32,8,1024]{2,1,0:T(8,128)(2,1)}) custom-call(bf16[1056,16,128]{2,1,0:T(8,128)(2,1)S(1)} %get-tuple-element.6.cache_in, bf16[32,8,1024]{2,1,0:T(8,128)(2,1)S(1)} %get-tuple-element.7.att_in), custom_call_target="tpu_custom_call" | custom-call | tf_op jit(solution)/shard_map/write_out/pallas_call | solution.py:435

commit v3 on v2

--- a/solution.py
+++ b/solution.py
@@ -24,11 +24,11 @@
 TURN_TILES = TURN // BLK
 SCALE2 = math.log2(math.e) / math.sqrt(HD)
 LOW = -1e30
-Y_STEPS = sum(d << (2 * i) for i, d in enumerate((2, 2, 1, 3, 1, 3, 0, 0)))
-C_STEPS = sum(d << i for i, d in enumerate((0, 1, 0, 1, 1, 0, 1, 0)))
+Y_STEPS = sum(d << (2 * i) for i, d in enumerate((0, 0, 2, 2, 1, 3, 1, 3)))
+C_STEPS = sum(d << i for i, d in enumerate((0, 1, 0, 1, 0, 1, 1, 0)))
 Z_ORDER = (4, 3, 5, 0, 2, 6, 1, 7)
 Z_STEPS = sum(d << (3 * i) for i, d in enumerate(Z_ORDER))
-SELF = (PLANES - 1) * NZ + Z_ORDER.index(0)
+SELF = Z_ORDER.index(0)
 PIECES = 8
 VMEM = 62148608
 
@@ -39,7 +39,7 @@
     anchor_v, delta_v, scale_v, slot_ref, recv_ref, q_v, kv_v, stage, spread, bias_v, inv_v, inv_ref,
     perm, qf, qsend, qarr, kvsend, kvarr, send, arr,
     flat, keys, values, acc, top, outsend, outarr,
-    load_sem, send_sem, recv_sem, turn_send, turn_recv, back_send, back_recv, inv_sem, out_sem,
+    load_sem, send_sem, recv_sem, turn_send, turn_recv, back_send, back_recv, inv_sem, out_sem, gate,
 ):
     store = lax.axis_index("store")
     x = lax.axis_index("tp")
@@ -49,8 +49,8 @@
         pltpu.make_async_copy(src, dst, load_sem.at[i])
         for i, (src, dst) in enumerate(
             (
-                (q_hbm, q_v), (kv_hbm, kv_v), (scale_hbm, scale_v), (slot_hbm, slot_ref),
-                (recv_hbm, recv_ref), (anchor_hbm, anchor_v), (delta_hbm, delta_v),
+                (scale_hbm, scale_v), (slot_hbm, slot_ref), (anchor_hbm, anchor_v),
+                (delta_hbm, delta_v), (q_hbm, q_v), (kv_hbm, kv_v), (recv_hbm, recv_ref),
             )
         )
     ]
@@ -59,17 +59,17 @@
 
     barrier = pltpu.get_barrier_semaphore()
 
-    me = store * NX + x
-    devices = NZ * NY * NC * NX
-
-    def greet(i, _):
-        other = (me + 1 + i) & (devices - 1)
-        pl.semaphore_signal(
-            barrier, inc=1, device_id=(other >> 2, other & 3), device_id_type=MESH
-        )
-        return 0
-
-    lax.fori_loop(0, devices - 1, greet, 0, unroll=15)
+    def on_line(n):
+        z2, core2 = (z + (n >> 1)) & (NZ - 1), (core + (n & 1)) & (NC - 1)
+        return ((z2 * NY + y) * NC + core2, x)
+
+    def in_group(n):
+        y2, x2 = (y + (n >> 2)) & (NY - 1), (x + (n & 3)) & (NX - 1)
+        return ((z * NY + y2) * NC + core, x2)
+
+    for n in range(1, 16):
+        pl.semaphore_signal(barrier, inc=1, device_id=on_line(n), device_id_type=MESH)
+        pl.semaphore_signal(barrier, inc=1, device_id=in_group(n), device_id_type=MESH)
 
     out_row = lax.broadcasted_iota(jnp.int32, (64, 64), 0)
     in_row = lax.broadcasted_iota(jnp.int32, (64, 64), 1)
@@ -80,7 +80,7 @@
         wide = jnp.concatenate(tiles, axis=1).astype(jnp.bfloat16)
         return jnp.dot(perm[...], wide, preferred_element_type=jnp.float32).astype(jnp.bfloat16)
 
-    loads[2].wait()
+    loads[0].wait()
     scale = scale_v[...].astype(jnp.float32)
     slots = scale.shape[2]
     for kv in range(2):
@@ -93,27 +93,9 @@
             column = flat[part + kv * 8 : part + kv * 8 + 8, lane : lane + 1]
             spread[kv, slot] = jnp.broadcast_to(column, (8, HD))
 
-    loads[0].wait()
-    for q in range(QPG):
-        lanes = q_v[:, :, q * HD : (q + 1) * HD].astype(jnp.float32)
-        qf[q] = lanes.reshape(TOK * 8, HD)
-        for h in range(8):
-            rows = qf[q, pl.ds(h, TOK, stride=8), :]
-            qsend[h // 2, h % 2, q * TOK : (q + 1) * TOK, :] = rows.astype(jnp.bfloat16)
-    loads[1].wait()
-    turn_blocks = []
-    for b in range(TOK // BLK):
-        parts = []
-        for r in range(BLK):
-            row = kv_v[b * BLK + r].astype(jnp.float32)
-            parts += [row[:, :HD], row[:, HD:]]
-        turn_blocks.append(jnp.concatenate(parts, axis=0))
-    mixed = split(turn_blocks)
-    for t in range(NX):
-        for b in range(TOK // BLK):
-            kvsend[t, b] = mixed[t * 16 : (t + 1) * 16, b * HD : (b + 1) * HD]
-
-    pl.semaphore_wait(barrier, devices - 1)
+    pl.semaphore_wait(barrier, 30)
+    for n in range(1, 16):
+        pl.semaphore_signal(gate, inc=1, device_id=in_group(n), device_id_type=MESH)
 
     def turn_copies(d):
         to = lax.rem(x + d, NX)
@@ -128,7 +110,7 @@
             ),
         )
 
-    for load in loads[3:]:
+    for load in loads[1:4]:
         load.wait()
 
     def offsets(j):
@@ -137,12 +119,24 @@
     def z_offset(i):
         return (Z_STEPS >> (3 * i)) & (NZ - 1)
 
-    def send_session(k, _):
+    def target(k):
         j, i = k >> 3, k & 7
         dy, dc = offsets(j)
         z2, y2, core2 = (z + z_offset(i)) & (NZ - 1), (y + dy) & (NY - 1), (core + dc) & (NC - 1)
-        session = (z2 * NY + y2) * NC + core2
-        box = j + jnp.where(k >= (PLANES - 1) * NZ + NZ // 2, 1, 0)
+        return (z2 * NY + y2) * NC + core2
+
+    mine = (y * NC + core) * PER_STEP + z * NX + x
+
+    def block_copy(k, d):
+        to = (x + d) & (NX - 1)
+        box = (k >> 3) + jnp.where(k >= (PLANES - 1) * NZ + NZ // 2, 1, 0)
+        return pltpu.make_async_remote_copy(
+            send.at[k, to], arr.at[mine], send_sem.at[k >> 3], recv_sem.at[box],
+            device_id=(target(k), to), device_id_type=MESH,
+        )
+
+    def decode(k):
+        session = target(k)
         tiles = []
         for c in range(CAP):
             slot = jnp.maximum(slot_ref[c, 0, session], 0)
@@ -158,31 +152,53 @@
         for t in range(NX):
             for c in range(CAP):
                 send[k, t, c] = mixed[t * 16 : (t + 1) * 16, c * HD : (c + 1) * HD]
-        mine = (y * NC + core) * PER_STEP + z * NX + x
+
+    def send_line(k, _):
+        decode(k)
+        pl.when(k != SELF)(block_copy(k, 0).start)
+        return 0
+
+    def send_rest(k, _):
+        for d in range(1, NX):
+            block_copy(k, d).start()
+        return 0
+
+    def send_all(k, _):
+        decode(k)
         for d in range(NX):
-            to = (x + d) & (NX - 1)
-            copy = pltpu.make_async_remote_copy(
-                send.at[k, to], arr.at[mine], send_sem.at[j], recv_sem.at[box],
-                device_id=(session, to), device_id_type=MESH,
-            )
-            if d:
-                copy.start()
-            else:
-                pl.when(k != SELF)(copy.start)
-
-        @pl.when(k == SELF)
-        def _():
-            arr[mine] = send[SELF, x]
-
-        return 0
-
-    lax.fori_loop(0, NZ, send_session, 0)
+            block_copy(k, d).start()
+        return 0
+
+    lax.fori_loop(0, 2 * NZ, send_line, 0)
+    arr[mine] = send[SELF, x]
+    pl.semaphore_wait(gate, 15)
+    lax.fori_loop(0, 2 * NZ, send_rest, 0)
+    loads[4].wait()
+    for q in range(QPG):
+        lanes = q_v[:, :, q * HD : (q + 1) * HD].astype(jnp.float32)
+        qf[q] = lanes.reshape(TOK * 8, HD)
+        for h in range(8):
+            rows = qf[q, pl.ds(h, TOK, stride=8), :]
+            qsend[h // 2, h % 2, q * TOK : (q + 1) * TOK, :] = rows.astype(jnp.bfloat16)
+    loads[5].wait()
+    turn_blocks = []
+    for b in range(TOK // BLK):
+        parts = []
+        for r in range(BLK):
+            row = kv_v[b * BLK + r].astype(jnp.float32)
+            parts += [row[:, :HD], row[:, HD:]]
+        turn_blocks.append(jnp.concatenate(parts, axis=0))
+    mixed = split(turn_blocks)
+    for t in range(NX):
+        for b in range(TOK // BLK):
+            kvsend[t, b] = mixed[t * 16 : (t + 1) * 16, b * HD : (b + 1) * HD]
     for d in range(1, NX):
         for copy in turn_copies(d):
             copy.start()
     qarr[x] = qsend[x]
     kvarr[x] = kvsend[x]
-    lax.fori_loop(NZ, PLANES * NZ, send_session, 0)
+    lax.fori_loop(2 * NZ, PLANES * NZ, send_all, 0)
+    loads[6].wait()
 
     recv_rows = [recv_ref[c] for c in range(CAP)]
     dead = [jnp.where(row >= 0, 0.0, 1.0) for row in recv_rows]
@@ -294,26 +310,26 @@
         attend(receive(j, j, PER_STEP, 0, NZ))
         return 0
 
-    lax.fori_loop(0, PLANES - 1, step, 0)
+    attend(receive(0, 0, PER_STEP - 1, 0, NZ))
+    lax.fori_loop(1, PLANES - 1, step, 0)
     last, half = PLANES - 1, NZ // 2
-    attend(receive(last, last, PER_STEP // 2 - 1, 0, half))
+    attend(receive(last, last, PER_STEP // 2, 0, half))
     bias = receive(last, last + 1, PER_STEP // 2, half, NZ)
-    def back_copy(d):
-        to = lax.rem(x + d, NX)
+    def back_copy(d, h):
+        to = (x + d) & (NX - 1)
         return pltpu.make_async_remote_copy(
-            outsend.at[to], outarr.at[x], back_send.at[d - 1], back_recv.at[d - 1],
+            outsend.at[to, h], outarr.at[x, h], back_send.at[d - 1, h], back_recv.at[d - 1, h],
             device_id=(store, to), device_id_type=MESH,
         )
 
     for d in (2, 1, 3, 0):
-        g = lax.rem(x + d, NX)
+        g = (x + d) & (NX - 1)
         for h in range(HEADS):
             total, _ = update(bias, h, g)
             outsend[g, h] = (total[:, :HD] / total[:, HD:]).astype(jnp.bfloat16)
-        if d:
-            back_copy(d).start()
-        else:
-            outarr[x] = outsend[x]
+            if d:
+                back_copy(d, h).start()
+    outarr[x] = outsend[x]
 
     inv_copy.wait()
 
@@ -337,7 +353,8 @@
         moves[p].start()
 
     for d in range(1, NX):
-        back_copy(d).wait()
+        for h in range(HEADS):
+            back_copy(d, h).wait()
     for t in range(NX):
         for hh in range(HEADS):
             for q in range(QPG):
@@ -350,7 +367,7 @@
     for move in moves:
         move.wait()
     for j in range(PLANES):
-        count = PER_STEP - 1 if j == last else PER_STEP
+        count = PER_STEP - 1 if j == 0 else PER_STEP
         span = arr.at[pl.ds(0, count)]
         pltpu.make_async_remote_copy(
             span, span, send_sem.at[j], recv_sem.at[j],
@@ -419,10 +436,11 @@
             pltpu.SemaphoreType.DMA((PLANES + 1,)),
             pltpu.SemaphoreType.DMA((2, NX - 1)),
             pltpu.SemaphoreType.DMA((2, NX - 1)),
-            pltpu.SemaphoreType.DMA((NX - 1,)),
-            pltpu.SemaphoreType.DMA((NX - 1,)),
+            pltpu.SemaphoreType.DMA((NX - 1, HEADS)),
+            pltpu.SemaphoreType.DMA((NX - 1, HEADS)),
             pltpu.SemaphoreType.DMA,
             pltpu.SemaphoreType.DMA((PIECES,)),
+            pltpu.SemaphoreType.REGULAR,
         ],
         compiler_params=pltpu.CompilerParams(
             collective_id=0, has_side_effects=True, vmem_limit_bytes=VMEM

time: 143 us -> 144 us (level)
  no operation moved by 1% of the time
where the time goes in v3:
time: 144 us; the launch traced here: 143 us
  Pallas kernels  143 us (99%)
    pallas_call x1, Pallas kernels, shards(): pl.pallas_call(body, out_shape=(pltpu.VMEM(cache_shape, bf16), pltpu.VMEM...  140 us

profile of v3, /device:TPU:1, one launch (start us, length us, event | category | flops | bytes accessed | tf_op | source)
XLA Modules:
  0.0 143.5 jit_solution(5827826670989739471)
XLA Ops:
  0.6 140.4 %restore_attend.1 = (bf16[1056,16,128]{2,1,0:T(8,128)(2,1)S(1)}, bf16[32,8,1024]{2,1,0:T(8,128)(2,1)S(1)}) custom-call(bf16[320,8,256]{2,1,0:T(8,128)(2,1)} %anchor_hbm.1, bf16[320,4,8,256]{3,2,1,0:T(8,128)(2,1)} %delta_hbm.1, bf16[8,2,320]{2,1,0:T(2,128)(2,1)} %bitcast.8, s32[5,1,64]{2,1,0:T(1,128)} %bitcast.10, s32[5,1,256]{2,1,0:T(1,128)} %bitcast.9, ...), custom_call_target="tpu_custom_call" | custom-call | tf_op jit(solution)/shard_map/restore_attend/pallas_call | solution.py:396
  141.1 2.2 %write_out.1 = (bf16[1056,16,128]{2,1,0:T(8,128)(2,1)}, bf16[32,8,1024]{2,1,0:T(8,128)(2,1)}) custom-call(bf16[1056,16,128]{2,1,0:T(8,128)(2,1)S(1)} %get-tuple-element.6.cache_in, bf16[32,8,1024]{2,1,0:T(8,128)(2,1)S(1)} %get-tuple-element.7.att_in), custom_call_target="tpu_custom_call" | custom-call | tf_op jit(solution)/shard_map/write_out/pallas_call | solution.py:453

commit v4 on v3

--- a/solution.py
+++ b/solution.py
@@ -131,7 +131,7 @@
         to = (x + d) & (NX - 1)
         box = (k >> 3) + jnp.where(k >= (PLANES - 1) * NZ + NZ // 2, 1, 0)
         return pltpu.make_async_remote_copy(
-            send.at[k, to], arr.at[mine], send_sem.at[k >> 3], recv_sem.at[box],
+            send.at[k, to], arr.at[pl.ds(mine * CAP, CAP)], send_sem.at[k >> 3], recv_sem.at[box],
             device_id=(target(k), to), device_id_type=MESH,
         )
 
@@ -169,8 +169,8 @@
             block_copy(k, d).start()
         return 0
 
-    lax.fori_loop(0, 2 * NZ, send_line, 0)
-    arr[mine] = send[SELF, x]
+    lax.fori_loop(0, 2 * NZ, send_line, 0, unroll=4)
+    arr[pl.ds(mine * CAP, CAP)] = send[SELF, x]
     pl.semaphore_wait(gate, 15)
     lax.fori_loop(0, 2 * NZ, send_rest, 0)
     loads[4].wait()
@@ -197,7 +197,7 @@
             copy.start()
     qarr[x] = qsend[x]
     kvarr[x] = kvsend[x]
-    lax.fori_loop(2 * NZ, PLANES * NZ, send_all, 0)
+    lax.fori_loop(2 * NZ, PLANES * NZ, send_all, 0, unroll=4)
     loads[6].wait()
 
     recv_rows = [recv_ref[c] for c in range(CAP)]
@@ -226,7 +226,7 @@
         recv_rows + [jnp.full((8 - CAP, PER_STEP * PLANES), -1, jnp.int32)], axis=0
     ).T
     holder = lax.broadcasted_iota(jnp.int32, (PER_STEP * PLANES, 1), 0)
-    place_of = (((holder >> 2) & 7) * PER_STEP + (holder >> 5) * NX + (holder & 3)) * 8
+    place_of = (((holder >> 2) & 7) * PER_STEP + (holder >> 5) * NX + (holder & 3)) * CAP
     for part in range(NBLK // HD):
         block = lax.broadcasted_iota(jnp.int32, (PER_STEP * PLANES, HD), 1) + part * HD
         found = jnp.zeros((PER_STEP * PLANES, HD), jnp.int32)
@@ -268,18 +268,19 @@
             top[h, g] = jnp.broadcast_to(peak, (ROWS, HD))
 
     def receive(j, box, count, z_from, z_to):
-        first = origin(j) * PER_STEP
-        span = arr.at[pl.ds(0, count)]
+        first = origin(j) * (PER_STEP * CAP)
+        span = arr.at[pl.ds(0, count * CAP)]
         pltpu.make_async_remote_copy(
             span, span, send_sem.at[0], recv_sem.at[box],
             device_id=(store, (x + 1) & (NX - 1)), device_id_type=MESH,
         ).wait_recv()
         lines = (z_to - z_from) * NX
         for i in range(z_from, z_to):
-            at = first + ((z - Z_ORDER[i]) & (NZ - 1)) * NX
-            for c in range(CAP):
-                tiles = arr[pl.ds(at, NX), c].reshape(NX * 16, HD).astype(jnp.float32)
-                flat[pl.ds((c * lines + (i - z_from) * NX) * 16, NX * 16), :] = tiles
+            at = first + ((z - Z_ORDER[i]) & (NZ - 1)) * (NX * CAP)
+            for n in range(NX):
+                for c in range(CAP):
+                    row = (c * lines + (i - z_from) * NX + n) * 16
+                    flat[row : row + 16, :] = arr[at + n * CAP + c].astype(jnp.float32)
         unpack(lines * CAP * BLK)
         rows = bias_v[j]
         return jnp.concatenate(
@@ -334,9 +335,7 @@
     inv_copy.wait()
 
     def place(b, _):
-        found = inv_ref[b >> 7, b & (HD - 1)]
-        source = jnp.clip(found >> 3, 0, PLANES * PER_STEP - 1)
-        stage[b] = arr[source, jnp.minimum(found & 7, CAP - 1)]
+        stage[b] = arr[inv_ref[b >> 7, b & (HD - 1)]]
         return 0
 
     many = (NBLK + TURN_TILES) // PIECES
@@ -368,7 +367,7 @@
         move.wait()
     for j in range(PLANES):
         count = PER_STEP - 1 if j == 0 else PER_STEP
-        span = arr.at[pl.ds(0, count)]
+        span = arr.at[pl.ds(0, count * CAP)]
         pltpu.make_async_remote_copy(
             span, span, send_sem.at[j], recv_sem.at[j],
             device_id=(store, (x + 1) & (NX - 1)), device_id_type=MESH,
@@ -423,7 +422,7 @@
             pltpu.VMEM((NX, TOK // BLK, 16, HD), bf16),
             pltpu.VMEM((NX, TOK // BLK, 16, HD), bf16),
             pltpu.VMEM((PLANES * NZ, NX, CAP, 16, HD), bf16),
-            pltpu.VMEM((PLANES * PER_STEP, CAP, 16, HD), bf16),
+            pltpu.VMEM((PLANES * PER_STEP * CAP, 16, HD), bf16),
             pltpu.VMEM((KEYS * 4, HD), f32),
             pltpu.VMEM((HEADS, KEYS, HD), bf16),
             pltpu.VMEM((HEADS, KEYS, 2 * HD), bf16),

time: 144 us -> 141 us (0.979)
  Pallas kernels: 143 us -> 140 us
    pallas_call x1, Pallas kernels: 140 us -> 137 us  [shards(): pl.pallas_call(body, out_shape=(pltpu.VMEM(cache_shape, bf16), pltpu.VMEM...]
where the time goes in v4:
time: 141 us; the launch traced here: 140 us
  Pallas kernels  140 us (99%)
    pallas_call x1, Pallas kernels, shards(): pl.pallas_call(body, out_shape=(pltpu.VMEM(cache_shape, bf16), pltpu.VMEM...  137 us

profile of v4, /device:TPU:1, one launch (start us, length us, event | category | flops | bytes accessed | tf_op | source)
XLA Modules:
  0.0 140.5 jit_solution(15593374596623510476)
XLA Ops:
  0.6 137.5 %restore_attend.1 = (bf16[1056,16,128]{2,1,0:T(8,128)(2,1)S(1)}, bf16[32,8,1024]{2,1,0:T(8,128)(2,1)S(1)}) custom-call(bf16[320,8,256]{2,1,0:T(8,128)(2,1)} %anchor_hbm.1, bf16[320,4,8,256]{3,2,1,0:T(8,128)(2,1)} %delta_hbm.1, bf16[8,2,320]{2,1,0:T(2,128)(2,1)} %bitcast.8, s32[5,1,64]{2,1,0:T(1,128)} %bitcast.10, s32[5,1,256]{2,1,0:T(1,128)} %bitcast.9, ...), custom_call_target="tpu_custom_call" | custom-call | tf_op jit(solution)/shard_map/restore_attend/pallas_call | solution.py:395
  138.1 2.2 %write_out.1 = (bf16[1056,16,128]{2,1,0:T(8,128)(2,1)}, bf16[32,8,1024]{2,1,0:T(8,128)(2,1)}) custom-call(bf16[1056,16,128]{2,1,0:T(8,128)(2,1)S(1)} %get-tuple-element.6.cache_in, bf16[32,8,1024]{2,1,0:T(8,128)(2,1)S(1)} %get-tuple-element.7.att_in), custom_call_target="tpu_custom_call" | custom-call | tf_op jit(solution)/shard_map/write_out/pallas_call | solution.py:452

commit v5 on v4

--- a/solution.py
+++ b/solution.py
@@ -54,7 +54,7 @@
             )
         )
     ]
-    for load in loads:
+    for load in loads[:4]:
         load.start()
 
     barrier = pltpu.get_barrier_semaphore()
@@ -112,6 +112,8 @@
 
     for load in loads[1:4]:
         load.wait()
+    for load in loads[4:]:
+        load.start()
 
     def offsets(j):
         return (Y_STEPS >> (2 * j)) & (NY - 1), (C_STEPS >> j) & (NC - 1)
@@ -129,7 +131,7 @@
 
     def block_copy(k, d):
         to = (x + d) & (NX - 1)
-        box = (k >> 3) + jnp.where(k >= (PLANES - 1) * NZ + NZ // 2, 1, 0)
+        box = (k >> 3) + jnp.where(k >= (PLANES - 1) * NZ + NZ * 3 // 4, 1, 0)
         return pltpu.make_async_remote_copy(
             send.at[k, to], arr.at[pl.ds(mine * CAP, CAP)], send_sem.at[k >> 3], recv_sem.at[box],
             device_id=(target(k), to), device_id_type=MESH,
@@ -313,9 +315,9 @@
 
     attend(receive(0, 0, PER_STEP - 1, 0, NZ))
     lax.fori_loop(1, PLANES - 1, step, 0)
-    last, half = PLANES - 1, NZ // 2
-    attend(receive(last, last, PER_STEP // 2, 0, half))
-    bias = receive(last, last + 1, PER_STEP // 2, half, NZ)
+    last, cut = PLANES - 1, NZ * 3 // 4
+    attend(receive(last, last, PER_STEP * 3 // 4, 0, cut))
+    bias = receive(last, last + 1, PER_STEP // 4, cut, NZ)
     def back_copy(d, h):
         to = (x + d) & (NX - 1)
         return pltpu.make_async_remote_copy(

time: 141 us -> 140 us (level)
  no operation moved by 1% of the time
where the time goes in v5:
time: 140 us
  Pallas kernels  139 us (99%)
    pallas_call x1, Pallas kernels, shards(): pl.pallas_call(body, out_shape=(pltpu.VMEM(cache_shape, bf16), pltpu.VMEM...  137 us

profile of v5, /device:TPU:1, one launch (start us, length us, event | category | flops | bytes accessed | tf_op | source)
XLA Modules:
  0.0 139.8 jit_solution(4421753776244338655)
XLA Ops:
  0.6 136.8 %restore_attend.1 = (bf16[1056,16,128]{2,1,0:T(8,128)(2,1)S(1)}, bf16[32,8,1024]{2,1,0:T(8,128)(2,1)S(1)}) custom-call(bf16[320,8,256]{2,1,0:T(8,128)(2,1)} %anchor_hbm.1, bf16[320,4,8,256]{3,2,1,0:T(8,128)(2,1)} %delta_hbm.1, bf16[8,2,320]{2,1,0:T(2,128)(2,1)} %bitcast.8, s32[5,1,64]{2,1,0:T(1,128)} %bitcast.10, s32[5,1,256]{2,1,0:T(1,128)} %bitcast.9, ...), custom_call_target="tpu_custom_call" | custom-call | tf_op jit(solution)/shard_map/restore_attend/pallas_call | solution.py:397
  137.4 2.2 %write_out.1 = (bf16[1056,16,128]{2,1,0:T(8,128)(2,1)}, bf16[32,8,1024]{2,1,0:T(8,128)(2,1)}) custom-call(bf16[1056,16,128]{2,1,0:T(8,128)(2,1)S(1)} %get-tuple-element.6.cache_in, bf16[32,8,1024]{2,1,0:T(8,128)(2,1)S(1)} %get-tuple-element.7.att_in), custom_call_target="tpu_custom_call" | custom-call | tf_op jit(solution)/shard_map/write_out/pallas_call | solution.py:454
